TPU v7x, 256 devices: a whole 4x4x8 slice. The times are simulated.
256 devices in a mesh: sample: 2 (over core), outer: 2 (over y_hi), inner: 64 (over y_lo, z, x).
Axes of the slice: x: 4, y: 4 (y_hi: 2, y_lo: 2; y = y_hi * 2 + y_lo), z: 8, core: 2. Of those that a mesh axis runs over, the one named last changes fastest.
Arguments:
- out_cotangent: bfloat16 [256, 384, 1152], P(('sample', 'outer', 'inner')), parts along dimension 0, may hold values from -6 to 6
- wo_spatial: bfloat16 [576, 1152], replicated, may hold values from -0.75 to 0.75
- wqkv_spatial: bfloat16 [1152, 1728], replicated, may hold values from -0.1875 to 0.1875
- wo_temporal: bfloat16 [576, 1152], replicated, may hold values from -0.75 to 0.75
- q_spatial: bfloat16 [256, 384, 576], P(('sample', 'outer', 'inner')), parts along dimension 0, may hold values from -6 to 6
- k_spatial: bfloat16 [256, 384, 576], P(('sample', 'outer', 'inner')), parts along dimension 0, may hold values from -6 to 6
- v_spatial: bfloat16 [256, 384, 576], P(('sample', 'outer', 'inner')), parts along dimension 0, may hold values from -6 to 6
- q_temporal: bfloat16 [256, 384, 576], P('sample', ('outer', 'inner')), parts along dimension 0, may hold values from -6 to 6
- k_temporal: bfloat16 [256, 384, 576], P('sample', ('outer', 'inner')), parts along dimension 0, may hold values from -6 to 6
- v_temporal: bfloat16 [256, 384, 576], P('sample', ('outer', 'inner')), parts along dimension 0, may hold values from -6 to 6
Outputs:
- middle_grad: bfloat16 [256, 384, 1152], P(('sample', 'outer', 'inner')), parts along dimension 0
- temporal_grads: bfloat16 [256, 384, 1728], P(('sample', 'outer', 'inner')), parts along dimension 0
There are 2 independent parts, one for each index of `sample`. A program takes and returns all parts, laid end to end along the dimension named above; an argument that names none is the same for every part. Nothing has to cross between parts.
All inputs are finite; a program needn't handle non-finite values.
Results may differ from a plain program's by a relative error of at most 0.015.
Values may be sent and summed in bfloat16 or wider, within the bound.
A program may use at most 64 MiB of HBM per device.

v0:
```python
import jax
import jax.numpy as jnp
from jax import lax
from jax.sharding import PartitionSpec as P

HEADS = 8


def attend_back(queries, key_rows, value_rows, grad_out):
    scaling = queries.shape[-1] ** (-0.5)
    scores = (
        jnp.einsum("lbhe,mbhe->bhlm", queries, key_rows, preferred_element_type=jnp.float32)
        * scaling
    )
    row_max = jnp.max(scores, axis=-1, keepdims=True)
    weights = jnp.exp(scores - row_max)
    weights = weights / jnp.sum(weights, axis=-1, keepdims=True)
    weights_low = weights.astype(jnp.bfloat16)
    grad_value = jnp.einsum(
        "bhlm,lbhe->mbhe", weights_low, grad_out, preferred_element_type=jnp.float32
    ).astype(jnp.bfloat16)
    grad_weight = jnp.einsum(
        "lbhe,mbhe->bhlm", grad_out, value_rows, preferred_element_type=jnp.float32
    )
    row_inner = jnp.sum(weights * grad_weight, axis=-1, keepdims=True)
    grad_score = (weights * (grad_weight - row_inner)).astype(jnp.bfloat16)
    grad_query = (
        jnp.einsum("bhlm,mbhe->lbhe", grad_score, key_rows, preferred_element_type=jnp.float32)
        * scaling
    ).astype(jnp.bfloat16)
    grad_key = (
        jnp.einsum("bhlm,lbhe->mbhe", grad_score, queries, preferred_element_type=jnp.float32)
        * scaling
    ).astype(jnp.bfloat16)
    return (grad_query, grad_key, grad_value)


def heads_view(array, length, batch):
    return array.reshape(length, batch, HEADS, array.shape[-1] // HEADS)


def local(
    out_cotangent,
    wo_spatial,
    wqkv_spatial,
    wo_temporal,
    q_spatial,
    k_spatial,
    v_spatial,
    q_temporal,
    k_temporal,
    v_temporal,
):
    tokens = out_cotangent.shape[1]
    features = out_cotangent.shape[2]
    channels = q_spatial.shape[2]
    contract = (((1,), (1,)), ((), ()))
    grad_rows = out_cotangent.reshape(tokens, features)
    spatial_out = lax.dot_general(
        grad_rows, wo_spatial, contract, preferred_element_type=jnp.float32
    ).astype(jnp.bfloat16)
    spatial_query, spatial_key, spatial_value = attend_back(
        heads_view(q_spatial, tokens, 1),
        heads_view(k_spatial, tokens, 1),
        heads_view(v_spatial, tokens, 1),
        heads_view(spatial_out, tokens, 1),
    )
    spatial_grads = jnp.concatenate(
        [
            spatial_query.reshape(tokens, channels),
            spatial_key.reshape(tokens, channels),
            spatial_value.reshape(tokens, channels),
        ],
        axis=1,
    )
    spatial_term = lax.dot_general(
        spatial_grads, wqkv_spatial, contract, preferred_element_type=jnp.float32
    )
    middle = (grad_rows.astype(jnp.float32) + spatial_term).astype(jnp.bfloat16)
    groups = lax.axis_size(("outer", "inner"))
    pos_dev = tokens // groups
    projected = lax.dot_general(
        middle, wo_temporal, contract, preferred_element_type=jnp.float32
    ).astype(jnp.bfloat16)
    temporal_out = lax.all_to_all(
        projected.reshape(groups, pos_dev, channels),
        ("outer", "inner"),
        split_axis=0,
        concat_axis=0,
        tiled=True,
    )
    frames = q_temporal.shape[0]
    temporal_query, temporal_key, temporal_value = attend_back(
        heads_view(q_temporal, frames, pos_dev),
        heads_view(k_temporal, frames, pos_dev),
        heads_view(v_temporal, frames, pos_dev),
        heads_view(temporal_out, frames, pos_dev),
    )
    stacked = jnp.concatenate(
        [
            temporal_query.reshape(frames, pos_dev, channels),
            temporal_key.reshape(frames, pos_dev, channels),
            temporal_value.reshape(frames, pos_dev, channels),
        ],
        axis=2,
    )
    returned = lax.all_to_all(stacked, ("outer", "inner"), split_axis=0, concat_axis=0, tiled=True)
    return (middle.reshape(1, tokens, features), returned.reshape(1, tokens, 3 * channels))


def solution(mesh):
    return jax.shard_map(
        local,
        mesh=mesh,
        in_specs=(
            P(("sample", "outer", "inner"), None, None),
            P(),
            P(),
            P(),
            P(("sample", "outer", "inner"), None, None),
            P(("sample", "outer", "inner"), None, None),
            P(("sample", "outer", "inner"), None, None),
            P("sample", ("outer", "inner"), None),
            P("sample", ("outer", "inner"), None),
            P("sample", ("outer", "inner"), None),
        ),
        out_specs=(
            P(("sample", "outer", "inner"), None, None),
            P(("sample", "outer", "inner"), None, None),
        ),
        check_vma=False,
    )
```

profile of v0, /device:TPU:32, one launch (start us, length us, event | category | flops | bytes accessed | tf_op | source)
XLA Modules:
  0.0 129.2 jit_solution(7732414844781540091)
XLA Ops:
  0.7 5.0 %fusion.31 = (f32[8,384]{1,0:T(8,128)S(1)}, f32[8,384,384]{1,2,0:T(8,128)}) fusion(bf16[384,8,72]{0,2,1:T(8,128)(2,1)} %bitcast.69, bf16[384,8,72]{0,2,1:T(8,128)(2,1)} %bitcast.71), kind=kOutput, calls=%fused_computation.43 | convolution fusion | flops 173408640 | bytes 5615616 | tf_op jit(solution)/shard_map/sub | solution.py:16
  5.6 0.9 convolution_convert_fusion.2
  6.6 3.3 %multiply_reduce_fusion = (f32[8,384]{1,0:T(8,128)S(1)}, f32[8,384,384]{1,2,0:T(8,128)S(1)}) fusion(f32[8,384,384]{1,2,0:T(8,128)} %get-tuple-element.5, f32[8,384]{1,0:T(8,128)S(1)} %get-tuple-element.4, bf16[384,8,72]{0,2,1:T(8,128)(2,1)S(1)} %bitcast.85, bf16[384,8,72]{0,2,1:T(8,128)(2,1)S(1)} %bitcast.82), kind=kOutput, calls=%fused_computation.3 | convolution fusion | flops 173405184 | bytes 10346496 | tf_op jit(solution)/shard_map/lbhe,mbhe->bhlm/dot_general | solution.py:22
  10.3 0.7 multiply_convert_fusion
  11.0 0.3 copy-done.3
  11.3 1.1 fusion.20
  12.4 0.5 fusion.19
  12.9 1.1 fusion.16
  14.0 1.0 copy-done.9
  15.0 2.0 %fusion.5 = bf16[384,1152]{1,0:T(8,128)(2,1)S(1)} fusion(bf16[1152,1728]{0,1:T(8,128)(2,1)S(1)} %copy-done.9, bf16[384,576]{0,1:T(8,128)(2,1)S(1)} %bitcast.87, bf16[384,576]{0,1:T(8,128)(2,1)S(1)} %bitcast.77, bf16[384,576]{0,1:T(8,128)(2,1)S(1)} %bitcast.78, bf16[1,384,1152]{2,1,0:T(8,128)(2,1)S(1)} %copy-done.11), kind=kOutput, calls=%fused_computation.8 | convolution fusion | flops 1534132224 | bytes 7077888 | tf_op jit(solution)/shard_map/dot_general | solution.py:76
  17.1 0.9 copy-done.13
  18.0 0.9 convolution_convert_fusion.1
  18.9 0.3 copy.23
  19.1 1.1 reshape.128
  20.2 15.0 %all-to-all-start = ((bf16[128,3,576]{2,1,0:T(4,128)(2,1)}), bf16[128,3,576]{2,1,0:T(4,128)(2,1)S(1)}, u32[]{:S(2)}, u32[]{:S(2)}) async-start(bf16[128,3,576]{2,1,0:T(4,128)(2,1)} %reshape.128), calls=%async_computation | async-start | bytes 1310720 | tf_op jit(solution)/shard_map/all_to_all | solution.py:85
  35.2 2.5 %fusion.32 = (f32[3,8,128]{2,1,0:T(8,128)}, f32[3,8,128,128]{2,3,1,0:T(8,128)S(1)}) fusion(bf16[128,3,8,72]{0,3,2,1:T(8,128)(2,1)} %bitcast.75, bf16[128,3,8,72]{0,3,2,1:T(8,128)(2,1)} %bitcast.73), kind=kOutput, calls=%fused_computation.44 | convolution fusion | flops 57802880 | bytes 2469888 | tf_op jit(solution)/shard_map/sub | solution.py:16
  37.7 19.4 %all-to-all-done = bf16[128,3,576]{2,1,0:T(4,128)(2,1)S(1)} async-done(((bf16[128,3,576]{2,1,0:T(4,128)(2,1)}), bf16[128,3,576]{2,1,0:T(4,128)(2,1)S(1)}, u32[]{:S(2)}, u32[]{:S(2)}) %all-to-all-start) | async-done | bytes 442400 | tf_op jit(solution)/shard_map/all_to_all | solution.py:85
  57.1 1.3 copy.24
  58.3 1.6 %multiply_reduce_fusion.2 = (f32[3,8,128]{2,1,0:T(8,128)S(1)}, f32[3,8,128,128]{2,3,1,0:T(8,128)S(1)}) fusion(f32[3,8,128,128]{2,3,1,0:T(8,128)S(1)} %get-tuple-element.9, f32[3,8,128]{2,1,0:T(8,128)} %get-tuple-element.8, bf16[128,3,8,72]{0,3,2,1:T(8,128)(2,1)} %bitcast.79, bf16[128,3,8,72]{0,3,2,1:T(8,128)(2,1)} %bitcast.83), kind=kOutput, calls=%fused_computation.15 | convolution fusion | flops 57799680 | bytes 4055040 | tf_op jit(solution)/shard_map/lbhe,mbhe->bhlm/dot_general | solution.py:22
  60.0 0.4 multiply_convert_fusion.1
  60.4 0.6 copy-done.5
  61.0 0.4 fusion.21
  61.4 0.7 fusion.22
  62.1 0.4 copy-done.2
  62.5 1.5 %convolution_convert_fusion = bf16[3,8,72,128]{3,2,1,0:T(8,128)(2,1)} fusion(bf16[128,3,8,72]{0,3,2,1:T(8,128)(2,1)S(1)} %bitcast.80, f32[3,8,128,128]{2,3,1,0:T(8,128)S(1)} %copy-done.2, f32[3,8,128]{2,1,0:T(8,128)S(1)} %copy-done.8), kind=kOutput, calls=%fused_computation.28 | convolution fusion | flops 57630720 | bytes 2469888 | tf_op jit(solution)/shard_map/bhlm,lbhe->mbhe/dot_general | solution.py:19
  64.0 0.7 copy.28
  64.7 0.8 copy.29
  65.5 1.6 %copy.30 = bf16[128,3,576]{2,1,0:T(4,128)(2,1)S(1)} copy(bf16[128,3,576]{0,2,1:T(8,128)(2,1)} %bitcast.81) | data formatting | bytes 884736 | tf_op jit(solution)/shard_map/reshape | solution.py:103
  67.0 4.4 %concatenate.7 = bf16[128,3,1728]{2,1,0:T(4,128)(2,1)} concatenate(bf16[128,3,576]{2,1,0:T(4,128)(2,1)S(1)} %copy.28, bf16[128,3,576]{2,1,0:T(4,128)(2,1)S(1)} %copy.29, bf16[128,3,576]{2,1,0:T(4,128)(2,1)S(1)} %copy.30), dimensions={2} | concatenate | bytes 2654208 | tf_op jit(solution)/shard_map/concatenate | solution.py:99
  71.5 52.9 %all_to_all.10 = bf16[128,3,1728]{2,1,0:T(4,128)(2,1)S(1)} all-to-all(bf16[128,3,1728]{2,1,0:T(4,128)(2,1)} %concatenate.7), channel_id=1, replica_groups=mesh['sample'=2,'outer'=2,'inner'=64] {'outer','inner'}, dimensions={0} | all-to-all | bytes 2654208 | tf_op jit(solution)/shard_map/all_to_all | solution.py:107
  124.3 2.4 %reshape.134 = bf16[1,384,1728]{2,1,0:T(8,128)(2,1)} reshape(bf16[128,3,1728]{2,1,0:T(4,128)(2,1)S(1)} %all_to_all.10) | data formatting | bytes 2654208 | tf_op jit(solution)/shard_map/reshape | solution.py:108
  126.7 2.5 %copy.31 = bf16[1,384,1728]{1,2,0:T(8,128)(2,1)} copy(bf16[1,384,1728]{2,1,0:T(8,128)(2,1)} %reshape.134) | data formatting | bytes 2654208
  (28 shorter events, 0.5 us)
Async XLA Ops:
  0.6 5.0 %copy-start = (bf16[576,1152]{1,0:T(8,128)(2,1)S(1)}, bf16[576,1152]{1,0:T(8,128)(2,1)}, u32[]{:S(2)}) copy-start(bf16[576,1152]{1,0:T(8,128)(2,1)} %param.11) | copy-start | bytes 3981316
  0.6 5.0 %copy-start.11 = (bf16[1,384,1152]{2,1,0:T(8,128)(2,1)S(1)}, bf16[1,384,1152]{2,1,0:T(8,128)(2,1)}, u32[]{:S(2)}) copy-start(bf16[1,384,1152]{2,1,0:T(8,128)(2,1)} %param.10) | copy-start | bytes 2654212
  5.6 1.0 copy-start.12
  6.5 3.6 %slice-start = ((s8[4718592]{0:T(1024)(128)(4,1)}), s8[4194304]{0:T(1024)(128)(4,1)S(1)}, s32[]{:S(2)}) async-start(s8[4718592]{0:T(1024)(128)(4,1)} %bitcast.65), calls=%async_computation.2 | async-start | bytes 8388608
  6.6 3.6 %slice-start.1 = ((s8[4718592]{0:T(1024)(128)(4,1)}), s8[524288]{0:T(1024)(128)(4,1)S(1)}, s32[]{:S(2)}) async-start(s8[4718592]{0:T(1024)(128)(4,1)} %bitcast.65), calls=%async_computation.3 | async-start | bytes 1048576
  10.3 1.0 copy-start.3
  11.3 1.1 copy-start.4
  12.9 2.1 %copy-start.9 = (bf16[1152,1728]{0,1:T(8,128)(2,1)S(1)}, bf16[1152,1728]{0,1:T(8,128)(2,1)}, u32[]{:S(2)}) copy-start(bf16[1152,1728]{0,1:T(8,128)(2,1)} %param.12) | copy-start | bytes 11943940
  15.0 3.0 %copy-start.10 = (bf16[576,1152]{1,0:T(8,128)(2,1)S(1)}, bf16[576,1152]{1,0:T(8,128)(2,1)}, u32[]{:S(2)}) copy-start(bf16[576,1152]{1,0:T(8,128)(2,1)} %param.13) | copy-start | bytes 3981316
  17.1 0.9 copy-start.13
  20.2 36.9 %all-to-all-start = ((bf16[128,3,576]{2,1,0:T(4,128)(2,1)}), bf16[128,3,576]{2,1,0:T(4,128)(2,1)S(1)}, u32[]{:S(2)}, u32[]{:S(2)}) async-start(bf16[128,3,576]{2,1,0:T(4,128)(2,1)} %reshape.128), calls=%async_computation | async-start | bytes 1310720 | tf_op jit(solution)/shard_map/all_to_all | solution.py:85
  37.7 22.2 %copy-start.1 = (f32[3,8,128,128]{2,3,1,0:T(8,128)}, f32[3,8,128,128]{2,3,1,0:T(8,128)S(1)}, u32[]{:S(2)}) copy-start(f32[3,8,128,128]{2,3,1,0:T(8,128)S(1)} %get-tuple-element.9) | copy-start | bytes 4718596
  58.3 1.6 %copy-start.8 = (f32[3,8,128]{2,1,0:T(8,128)S(1)}, f32[3,8,128]{2,1,0:T(8,128)}, u32[]{:S(2)}) copy-start(f32[3,8,128]{2,1,0:T(8,128)} %get-tuple-element.8) | copy-start | bytes 36868
  60.0 1.0 copy-start.5
  60.0 1.4 %copy-start.6 = (bf16[128,3,576]{0,2,1:T(8,128)(2,1)S(1)}, bf16[128,3,576]{0,2,1:T(8,128)(2,1)}, u32[]{:S(2)}) copy-start(bf16[128,3,576]{0,2,1:T(8,128)(2,1)} %param.17) | copy-start | bytes 1327108
  61.0 1.4 %copy-start.2 = (f32[3,8,128,128]{2,3,1,0:T(8,128)S(1)}, f32[3,8,128,128]{2,3,1,0:T(8,128)}, u32[]{:S(2)}) copy-start(f32[3,8,128,128]{2,3,1,0:T(8,128)} %copy-done.1) | copy-start | bytes 4718596
  61.0 1.5 %copy-start.7 = (bf16[128,3,576]{0,2,1:T(8,128)(2,1)S(1)}, bf16[128,3,576]{0,2,1:T(8,128)(2,1)}, u32[]{:S(2)}) copy-start(bf16[128,3,576]{0,2,1:T(8,128)(2,1)} %copy.24) | copy-start | bytes 1327108
where the time goes:
time: 130 us; the launch traced here: 129 us
  blocking collectives  52.9 us (41%)
  matrix products  21.4 us (16%)
  waiting for transfers between devices  19.4 us (15%)
  local copies, waits for them, and re-layouts  18.6 us (14%)
  starting transfers between devices  15 us (12%)
    all_to_all x1, blocking collectives, local(): lax.all_to_all(stacked, ('outer', 'inner'), split_axis=0, concat_axis=0,...  52.9 us
    all_to_all x1, waiting for transfers between devices, local(): lax.all_to_all(projected.reshape(groups, pos_dev, channels), ('outer', 'i...  19.4 us
    all_to_all x1, starting transfers between devices, local(): lax.all_to_all(projected.reshape(groups, pos_dev, channels), ('outer', 'i...  15 us
    sub x2, matrix products, attend_back(): weights = jnp.exp(scores - row_max)  7.43 us
    unnamed x33, local copies, waits for them, and re-layouts  6.16 us
    dot_general x2, matrix products, attend_back(): jnp.einsum('lbhe,mbhe->bhlm', grad_out, value_rows, preferred_element_typ...  4.93 us
    concatenate x1, local copies, waits for them, and re-layouts, local(): jnp.concatenate([temporal_query.reshape(frames, pos_dev, channels), tempo...  4.43 us
  transfers between devices with their start and end apart: 1, of which 1 were waited for; matrix products, arithmetic and copies ran while one was open for 2% of the time, Pallas kernels for 0%

commit v1 on v0

v1 whole, which is shorter than its diff:
```python
import functools

import jax
import jax.numpy as jnp
from jax import lax
from jax.experimental import pallas as pl
from jax.experimental.pallas import tpu as pltpu
from jax.sharding import PartitionSpec as P

HEADS = 8
HEAD = 72
PAIR = 2 * HEAD
CH = HEADS * HEAD
PAIRS = HEADS // 2
TOKENS = 384
FRAMES = 128
POS = 3
FEATURES = 1152
SLOTS1 = 7
SLOTS2 = 21
CHUNKS1 = ((0, 3), (3, 7))
CHUNKS2 = ((0, 3), (3, 9), (9, 15), (15, 21))
SCALE = HEAD ** -0.5
LOG2E = 1.4426950408889634
F32 = jnp.float32
BF16 = jnp.bfloat16


def dot(a, b, ca, cb):
    return lax.dot_general(a, b, (((ca,), (cb,)), ((), ())), preferred_element_type=F32)


def nn(a, b):
    return dot(a, b, 1, 0)


def nt(a, b):
    return dot(a, b, 1, 1)


def tn(a, b):
    return dot(a, b, 0, 0)


def coords():
    outer, inner = lax.axis_index("outer"), lax.axis_index("inner")
    y = outer * 2 + lax.div(inner, 32)
    z = lax.rem(lax.div(inner, 4), 8)
    x = lax.rem(inner, 4)
    return y, z, x


def device(y, z, x):
    return (lax.axis_index("sample"), lax.div(y, 2), lax.rem(y, 2) * 32 + z * 4 + x)


def peer(step):
    y, z, x = coords()
    shift = lax.rem(step * 5, 128)
    ty = lax.rem(y + lax.div(shift, 32), 4)
    tz = lax.rem(z + lax.rem(lax.div(shift, 4), 8), 8)
    tx = lax.rem(x + lax.rem(shift, 4), 4)
    return (ty * 8 + tz) * 4 + tx, device(ty, tz, tx)


def my_index():
    return lax.axis_index("outer") * 64 + lax.axis_index("inner")


def enter():
    barrier = pltpu.get_barrier_semaphore()

    def body(step, carry):
        _, dev = peer(step)
        pl.semaphore_signal(barrier, inc=1, device_id=dev, device_id_type=pl.DeviceIdType.MESH)
        return carry

    lax.fori_loop(1, FRAMES, body, 0)


def entered():
    pl.semaphore_wait(pltpu.get_barrier_semaphore(), FRAMES - 1)


def send(stage, recv, send_sem, recv_sem, lo, hi):
    mine = pl.ds(pl.multiple_of(my_index() * 2, 2), 2)
    land = recv.at[lo:hi, mine]
    pltpu.make_async_copy(stage.at[lo:hi, mine], land, recv_sem).start()

    def body(step, carry):
        index, dev = peer(step)
        pltpu.make_async_remote_copy(
            src_ref=stage.at[lo:hi, pl.ds(pl.multiple_of(index * 2, 2), 2)],
            dst_ref=land,
            send_sem=send_sem,
            recv_sem=recv_sem,
            device_id=dev,
            device_id_type=pl.DeviceIdType.MESH,
        ).start()
        return carry

    lax.fori_loop(1, FRAMES, body, 0)


def arrived(recv, sem, lo, hi):
    pltpu.make_async_copy(recv.at[lo:hi], recv.at[lo:hi], sem).wait()


def sent(stage, sem):
    part = stage.at[:, : 2 * (FRAMES - 1)]
    pltpu.make_async_copy(part, part, sem).wait()


def softmax_t(scores):
    top = jnp.max(scores, axis=0, keepdims=True)
    weights = jnp.exp2((scores - top) * (SCALE * LOG2E))
    return weights * (1.0 / jnp.sum(weights, axis=0, keepdims=True))


def grads_t(weights, weights_low, query, key, value, grad):
    grad_value = nt(grad, weights_low)
    grad_weight = tn(value, grad)
    inner = jnp.sum(weights * grad_weight, axis=0, keepdims=True)
    grad_score = (weights * (grad_weight - inner)).astype(BF16)
    grad_query = nn(key, grad_score) * SCALE
    grad_key = nt(query, grad_score) * SCALE
    return grad_query, grad_key, grad_value


def kernel(
    cot_h, wos_h, w_h, wot_h, qs_h, ks_h, vs_h, qt_h, kt_h, vt_h,
    mid_o, out_o,
    cot, wos, w, wot, qs, ks, vs, qt, kt, vt,
    gs, sgt, sg, pt, gt, rt, e01, e20, e21, weave,
    stage1, recv1, stage2, recv2,
    in_sem, send1, recv1_sem, send2, recv2_sem,
):
    loads = []
    order = ((cot_h, cot), (wos_h, wos), (qs_h, qs), (ks_h, ks), (vs_h, vs), (w_h, w), (wot_h, wot), (qt_h, qt), (kt_h, kt), (vt_h, vt))
    for i, (src, dst) in enumerate(order):
        copy = pltpu.make_async_copy(src, dst, in_sem.at[i])
        copy.start()
        loads.append(copy)
    enter()

    row = lax.broadcasted_iota(jnp.int32, (2 * FRAMES, TOKENS), 0)
    col = lax.broadcasted_iota(jnp.int32, (2 * FRAMES, TOKENS), 1)
    half, index = row & 1, row >> 1
    e01[...] = (col == 3 * index + half).astype(F32).astype(BF16)
    e20[...] = ((col == 3 * index + 2) & (half == 0)).astype(F32).astype(BF16)
    e21[...] = ((col == 3 * index + 2) & (half == 1)).astype(F32).astype(BF16)
    row = lax.broadcasted_iota(jnp.int32, (2 * FRAMES, 2 * FRAMES), 0)
    col = lax.broadcasted_iota(jnp.int32, (2 * FRAMES, 2 * FRAMES), 1)
    weave[...] = (col == (row & 1) * FRAMES + (row >> 1)).astype(F32).astype(BF16)

    loads[0].wait()
    loads[1].wait()
    gs[...] = nt(wos[...], cot[...]).astype(BF16)
    for i in (2, 3, 4):
        loads[i].wait()

    def spatial(p, carry):
        rows = pl.ds(pl.multiple_of(p * PAIR, 16), PAIR)
        q2, k2, v2, g2 = qs[rows], ks[rows], vs[rows], gs[rows]
        outs = []
        for i in range(2):
            cut = slice(i * HEAD, (i + 1) * HEAD)
            q, k, v, g = q2[cut], k2[cut], v2[cut], g2[cut]
            weights = softmax_t(tn(k, q))
            outs.append(grads_t(weights, weights.astype(BF16), q, k, v, g))
        for kind in range(3):
            both = jnp.concatenate([outs[0][kind], outs[1][kind]], axis=0).astype(BF16)
            sgt[pl.ds(pl.multiple_of(kind * CH + p * PAIR, 16), PAIR)] = both
        return carry

    lax.fori_loop(0, PAIRS, spatial, 0)
    sg[...] = sgt[...].T
    loads[5].wait()

    def project(n, carry):
        cols = pl.ds(pl.multiple_of(n * 384, 128), 384)
        mid_o[:, cols] = (cot[:, cols].astype(F32) + nn(sg[...], w[:, cols])).astype(BF16)
        return carry

    lax.fori_loop(0, FEATURES // 384, project, 0)
    loads[6].wait()
    entered()

    low = nt(mid_o[...], wot[0:256]).astype(BF16)
    stage1[0] = nn(e01[...], low[:, 0:128]).astype(BF16)
    stage1[1] = nn(e01[...], low[:, 128:256]).astype(BF16)
    stage1[2] = (nn(e20[...], low[:, 0:128]) + nn(e21[...], low[:, 128:256])).astype(BF16)
    send(stage1, recv1, send1, recv1_sem.at[0], *CHUNKS1[0])
    high = nt(mid_o[...], wot[256:576]).astype(BF16)
    stage1[3] = nn(e01[...], high[:, 0:128]).astype(BF16)
    stage1[4] = nn(e01[...], high[:, 128:256]).astype(BF16)
    stage1[5] = (nn(e20[...], high[:, 0:128]) + nn(e21[...], high[:, 128:256])).astype(BF16)
    rest = high[:, 256:320]
    stage1[6] = jnp.concatenate([nn(e01[...], rest), nn(e20[...], rest)], axis=1).astype(BF16)
    send(stage1, recv1, send1, recv1_sem.at[1], *CHUNKS1[1])

    for i in (7, 8, 9):
        loads[i].wait()

    def prepare(i, carry):
        j, p = lax.div(i, PAIRS), lax.rem(i, PAIRS)
        rows = pl.ds(pl.multiple_of(p * PAIR, 16), PAIR)
        q2, k2 = qt[j, rows], kt[j, rows]
        for h in range(2):
            cut = slice(h * HEAD, (h + 1) * HEAD)
            pt[j, p, h] = softmax_t(tn(k2[cut], q2[cut]))
        return carry

    lax.fori_loop(0, POS * PAIRS, prepare, 0)

    def unpack1(base, c):
        for i in range(2):
            block = tn(recv1[base + i], weave[...]).astype(BF16)
            rows = slice((c + i) * 128, (c + i + 1) * 128)
            gt[0, rows] = block[:, :128]
            gt[1, rows] = block[:, 128:]
        block = tn(recv1[base + 2], weave[...]).astype(BF16)
        gt[2, c * 128 : (c + 1) * 128] = block[:, :128]
        gt[2, (c + 1) * 128 : (c + 2) * 128] = block[:, 128:]

    def temporal(p):
        def body(j, carry):
            rows = slice(p * PAIR, (p + 1) * PAIR)
            q2, k2, v2, g2 = qt[j, rows], kt[j, rows], vt[j, rows], gt[j, rows]
            outs = []
            for h in range(2):
                cut = slice(h * HEAD, (h + 1) * HEAD)
                weights = pt[j, p, h]
                outs.append(grads_t(weights, weights.astype(BF16), q2[cut], k2[cut], v2[cut], g2[cut]))
            for kind in range(3):
                both = jnp.concatenate([outs[0][kind], outs[1][kind]], axis=0).astype(BF16)
                rt[j, (p * 3 + kind) * PAIR : (p * 3 + kind + 1) * PAIR] = both
            return carry

        lax.fori_loop(0, POS, body, 0)

    def pack2(t, c):
        wide = min(128, 3 * CH - (c + 1) * 128)
        for i, width in ((0, 128), (1, wide)):
            rows = slice((c + i) * 128, (c + i) * 128 + width)
            both = jnp.concatenate([rt[0, rows], rt[1, rows]], axis=1)
            stage2[t + i, :, 0:width] = nt(weave[...], both).astype(BF16)
        first = nt(weave[:, :128], rt[2, c * 128 : (c + 1) * 128])
        second = nt(weave[:, 128:], rt[2, (c + 1) * 128 : (c + 1) * 128 + wide])
        if wide < 128:
            second = jnp.concatenate([second, jnp.zeros((2 * FRAMES, 128 - wide), F32)], axis=1)
        stage2[t + 2] = (first + second).astype(BF16)

    arrived(recv1, recv1_sem.at[0], *CHUNKS1[0])
    unpack1(0, 0)
    temporal(0)
    pack2(0, 0)
    send(stage2, recv2, send2, recv2_sem.at[0], *CHUNKS2[0])

    arrived(recv1, recv1_sem.at[1], *CHUNKS1[1])
    unpack1(3, 2)
    block = tn(recv1[6], weave[...]).astype(BF16)
    gt[0, 512:576] = block[:64, :128]
    gt[1, 512:576] = block[:64, 128:]
    gt[2, 512:576] = block[64:, :128]
    for p in range(1, PAIRS):
        temporal(p)
        lo, hi = CHUNKS2[p]
        for t in range(lo, hi, 3):
            pack2(t, t // 3 * 2)
        send(stage2, recv2, send2, recv2_sem.at[p], lo, hi)

    def put(c, block):
        start, width = c * 128, block.shape[0]
        at = start
        while at < start + width:
            unit = at // PAIR
            stop = min((unit + 1) * PAIR, start + width)
            p, kind = unit // 3, unit % 3
            dest = kind * CH + p * PAIR + at - unit * PAIR
            out_o[dest : dest + stop - at] = block[at - start : stop - start]
            at = stop

    def unpack2(t, c):
        wide = min(128, 3 * CH - (c + 1) * 128)
        pair = recv2[t + 2]
        put(c, (tn(recv2[t], e01[...]) + tn(pair, e20[...])).astype(BF16))
        last = (tn(recv2[t + 1], e01[...]) + tn(pair, e21[...])).astype(BF16)
        put(c + 1, last[:wide])

    for p in range(PAIRS):
        lo, hi = CHUNKS2[p]
        arrived(recv2, recv2_sem.at[p], lo, hi)
        for t in range(lo, hi, 3):
            unpack2(t, t // 3 * 2)
    sent(stage1, send1)
    sent(stage2, send2)


def local(cot, wos, wqkv, wot, qs, ks, vs, qt, kt, vt):
    def flip(a):
        return a[0].T

    def turn(a):
        return jnp.transpose(a, (1, 2, 0))

    vmem = pl.BlockSpec(memory_space=pltpu.VMEM)
    hbm = pl.BlockSpec(memory_space=pl.ANY)
    spatial = pltpu.VMEM((CH, TOKENS), BF16)
    temporal = pltpu.VMEM((POS, CH, FRAMES), BF16)
    pick = pltpu.VMEM((2 * FRAMES, TOKENS), BF16)
    middle, grads = pl.pallas_call(
        kernel,
        out_shape=(
            jax.ShapeDtypeStruct((TOKENS, FEATURES), BF16),
            jax.ShapeDtypeStruct((3 * CH, TOKENS), BF16),
        ),
        in_specs=[hbm] * 10,
        out_specs=(vmem, vmem),
        scratch_shapes=[
            pltpu.VMEM((TOKENS, FEATURES), BF16),
            pltpu.VMEM((CH, FEATURES), BF16),
            pltpu.VMEM((3 * CH, FEATURES), BF16),
            pltpu.VMEM((CH, FEATURES), BF16),
            spatial, spatial, spatial,
            temporal, temporal, temporal,
            spatial,
            pltpu.VMEM((3 * CH, TOKENS), BF16),
            pltpu.VMEM((TOKENS, 3 * CH), BF16),
            pltpu.VMEM((POS, PAIRS, 2, FRAMES, FRAMES), F32),
            temporal,
            pltpu.VMEM((POS, 3 * CH, FRAMES), BF16),
            pick, pick, pick,
            pltpu.VMEM((2 * FRAMES, 2 * FRAMES), BF16),
            pltpu.VMEM((SLOTS1, 2 * FRAMES, 128), BF16),
            pltpu.VMEM((SLOTS1, 2 * FRAMES, 128), BF16),
            pltpu.VMEM((SLOTS2, 2 * FRAMES, 128), BF16),
            pltpu.VMEM((SLOTS2, 2 * FRAMES, 128), BF16),
            pltpu.SemaphoreType.DMA((10,)),
            pltpu.SemaphoreType.DMA,
            pltpu.SemaphoreType.DMA((len(CHUNKS1),)),
            pltpu.SemaphoreType.DMA,
            pltpu.SemaphoreType.DMA((len(CHUNKS2),)),
        ],
        compiler_params=pltpu.CompilerParams(
            collective_id=0, has_side_effects=True, vmem_limit_bytes=56 << 20
        ),
        name="reward_backward",
    )(
        cot[0], wos, wqkv.T, wot,
        flip(qs), flip(ks), flip(vs),
        turn(qt), turn(kt), turn(vt),
    )
    return middle[None], grads.T[None]


def solution(mesh):
    frames = P(("sample", "outer", "inner"), None, None)
    positions = P("sample", ("outer", "inner"), None)
    return jax.shard_map(
        local,
        mesh=mesh,
        in_specs=(frames, P(), P(), P(), frames, frames, frames, positions, positions, positions),
        out_specs=(frames, frames),
        check_vma=False,
    )
```

time: 130 us -> 82.4 us (0.63)
  Pallas kernels: 0 us -> 77.7 us
  blocking collectives: 52.9 us -> 0 us
  matrix products: 21.4 us -> 0 us
  waiting for transfers between devices: 19.4 us -> 0 us
  local copies, waits for them, and re-layouts: 18.6 us -> 3.32 us
  starting transfers between devices: 15 us -> 0 us
    pallas_call x0 -> x1, Pallas kernels: none -> 77.7 us  [local(): pl.pallas_call(kernel, out_shape=(jax.ShapeDtypeStruct((TOKENS, FEATURES)...]
    all_to_all x1 -> x0, blocking collectives: 52.9 us -> none  [local(): lax.all_to_all(stacked, ('outer', 'inner'), split_axis=0, concat_axis=0,...]
    all_to_all x1 -> x0, waiting for transfers between devices: 19.4 us -> none  [local(): lax.all_to_all(projected.reshape(groups, pos_dev, channels), ('outer', 'i...]
    all_to_all x1 -> x0, starting transfers between devices: 15 us -> none  [local(): lax.all_to_all(projected.reshape(groups, pos_dev, channels), ('outer', 'i...]
    dot_general x11 -> x0, matrix products: 13.9 us -> none  [the longest x2 4.93 us: attend_back(): jnp.einsum('lbhe,mbhe->bhlm', grad_out, value_rows, preferred_element_typ...]
    sub x2 -> x0, matrix products: 7.43 us -> none  [attend_back(): weights = jnp.exp(scores - row_max)]
    reshape x5 -> x0, local copies, waits for them, and re-layouts: 6.49 us -> none  [the longest x1 2.36 us: local(): returned.reshape(1, tokens, 3 * channels)]
    concatenate x1 -> x0, local copies, waits for them, and re-layouts: 4.43 us -> none  [local(): jnp.concatenate([temporal_query.reshape(frames, pos_dev, channels), tempo...]
  transfers between devices with their start and end apart: 1 -> 0, of which waited for: 1 -> 0; matrix products, arithmetic and copies ran while one was open for 2% -> 0% of each run, Pallas kernels for 0% -> 0%
where the time goes in v1:
time: 82.4 us; the launch traced here: 81.7 us
  Pallas kernels  77.7 us (94%)
  local copies, waits for them, and re-layouts  3.32 us (4%)
    pallas_call x1, Pallas kernels, local(): pl.pallas_call(kernel, out_shape=(jax.ShapeDtypeStruct((TOKENS, FEATURES)...  77.7 us
    unnamed x4, local copies, waits for them, and re-layouts  3.32 us

profile of v1, /device:TPU:32, one launch (start us, length us, event | category | flops | bytes accessed | tf_op | source)
XLA Modules:
  0.0 81.7 jit_solution(13213669451421823521)
XLA Ops:
  0.6 77.7 %reward_backward.1 = (bf16[384,1152]{1,0:T(8,128)(2,1)}, bf16[1728,384]{1,0:T(8,128)(2,1)}) custom-call(bf16[384,1152]{1,0:T(8,128)(2,1)} %bitcast.20, bf16[576,1152]{1,0:T(8,128)(2,1)} %wos_h.1, bf16[1728,1152]{1,0:T(8,128)(2,1)} %bitcast.18, bf16[576,1152]{1,0:T(8,128)(2,1)} %wot_h.1, bf16[576,384]{1,0:T(8,128)(2,1)} %bitcast.22, ...), custom_call_target="tpu_custom_call" | custom-call | tf_op jit(solution)/shard_map/reward_backward/pallas_call | solution.py:312
  78.3 0.0 copy-start
  78.4 2.2 %copy.14 = bf16[1,384,1152]{2,1,0:T(8,128)(2,1)} copy(bf16[1,384,1152]{2,1,0:T(8,128)(2,1)} %bitcast.21) | data formatting | bytes 1769472
  80.6 0.0 copy-done
  80.6 1.1 %copy.15 = bf16[1,384,1728]{1,2,0:T(8,128)(2,1)} copy(bf16[1,384,1728]{1,2,0:T(8,128)(2,1)S(1)} %bitcast.19) | data formatting | bytes 2654208
Async XLA Ops:
  78.3 2.3 %copy-start = (bf16[1728,384]{1,0:T(8,128)(2,1)S(1)}, bf16[1728,384]{1,0:T(8,128)(2,1)}, u32[]{:S(2)}) copy-start(bf16[1728,384]{1,0:T(8,128)(2,1)} %get-tuple-element.5) | copy-start | bytes 3981316

commit v2 on v1

--- a/solution.py
+++ b/solution.py
@@ -51,55 +51,78 @@
 
 
 def device(y, z, x):
-    return (lax.axis_index("sample"), lax.div(y, 2), lax.rem(y, 2) * 32 + z * 4 + x)
-
-
-def peer(step):
-    y, z, x = coords()
-    shift = lax.rem(step * 5, 128)
-    ty = lax.rem(y + lax.div(shift, 32), 4)
-    tz = lax.rem(z + lax.rem(lax.div(shift, 4), 8), 8)
-    tx = lax.rem(x + lax.rem(shift, 4), 4)
-    return (ty * 8 + tz) * 4 + tx, device(ty, tz, tx)
+    return lax.axis_index("sample") * FRAMES + (y * 8 + z) * 4 + x
 
 
 def my_index():
     return lax.axis_index("outer") * 64 + lax.axis_index("inner")
 
 
+def greet(sem, line):
+    y, z, x = coords()
+    if line == "x":
+        peers = [(y, z, lax.rem(x + i, 4)) for i in range(1, 4)]
+    elif line == "y":
+        peers = [(lax.rem(y + i, 4), z, x) for i in range(1, 4)]
+    else:
+        peers = [(y, lax.rem(z + i, 8), x) for i in range(1, 8)]
+    for peer in peers:
+        pl.semaphore_signal(
+            sem, inc=1, device_id=device(*peer), device_id_type=pl.DeviceIdType.LOGICAL
+        )
+
+
 def enter():
     barrier = pltpu.get_barrier_semaphore()
-
-    def body(step, carry):
-        _, dev = peer(step)
-        pl.semaphore_signal(barrier, inc=1, device_id=dev, device_id_type=pl.DeviceIdType.MESH)
-        return carry
-
-    lax.fori_loop(1, FRAMES, body, 0)
-
-
-def entered():
-    pl.semaphore_wait(pltpu.get_barrier_semaphore(), FRAMES - 1)
+    for line in "zyx":
+        greet(barrier, line)
+
+
+def lines_entered(sem):
+    pl.semaphore_wait(pltpu.get_barrier_semaphore(), 13)
+    greet(sem, "x")
+
+
+def planes_entered(sems):
+    pl.semaphore_wait(sems.at[0], 3)
+    greet(sems.at[1], "y")
+
+
+def entered(sem):
+    pl.semaphore_wait(sem, 3)
 
 
 def send(stage, recv, send_sem, recv_sem, lo, hi):
-    mine = pl.ds(pl.multiple_of(my_index() * 2, 2), 2)
-    land = recv.at[lo:hi, mine]
-    pltpu.make_async_copy(stage.at[lo:hi, mine], land, recv_sem).start()
-
-    def body(step, carry):
-        index, dev = peer(step)
+    me = my_index()
+    sample = lax.axis_index("sample")
+    y, z, x = coords()
+    sign = 1 - 2 * sample
+    depth = [lax.rem(z + sign * i + 8, 8) * 4 for i in range(8)]
+    land = recv.at[lo:hi, pl.ds(pl.multiple_of(me * 2, 2), 2)]
+    pltpu.make_async_copy(stage.at[lo:hi, pl.ds(pl.multiple_of(me * 2, 2), 2)], land, recv_sem).start()
+
+    def one(across, away):
+        ty = lax.rem(y + sign * lax.div(across, 4) + 4, 4)
+        tx = lax.rem(x + sign * lax.rem(across, 4) + 4, 4)
+        index = ty * 32 + depth[away] + tx
         pltpu.make_async_remote_copy(
             src_ref=stage.at[lo:hi, pl.ds(pl.multiple_of(index * 2, 2), 2)],
             dst_ref=land,
             send_sem=send_sem,
             recv_sem=recv_sem,
-            device_id=dev,
-            device_id_type=pl.DeviceIdType.MESH,
+            device_id=sample * FRAMES + index,
+            device_id_type=pl.DeviceIdType.LOGICAL,
         ).start()
+
+    def body(turn, carry):
+        for i, away in enumerate((4, 1, 7, 2, 6, 3, 5)):
+            one(lax.rem(turn + 5 * i + 5, 16), away)
+        one(turn + 1, 0)
         return carry
 
-    lax.fori_loop(1, FRAMES, body, 0)
+    lax.fori_loop(0, 15, body, 0)
+    for i, away in enumerate((4, 1, 7, 2, 6, 3, 5)):
+        one((15 + 5 * i + 5) % 16, away)
 
 
 def arrived(recv, sem, lo, hi):
@@ -127,13 +150,22 @@
     return grad_query, grad_key, grad_value
 
 
+def picks(e01, e20, e21):
+    row = lax.broadcasted_iota(jnp.int32, (2 * FRAMES, TOKENS), 0)
+    col = lax.broadcasted_iota(jnp.int32, (2 * FRAMES, TOKENS), 1)
+    half, index = row & 1, row >> 1
+    e01[...] = (col == 3 * index + half).astype(F32).astype(BF16)
+    e20[...] = ((col == 3 * index + 2) & (half == 0)).astype(F32).astype(BF16)
+    e21[...] = ((col == 3 * index + 2) & (half == 1)).astype(F32).astype(BF16)
+
+
 def kernel(
     cot_h, wos_h, w_h, wot_h, qs_h, ks_h, vs_h, qt_h, kt_h, vt_h,
-    mid_o, out_o,
+    mid_o, recv2,
     cot, wos, w, wot, qs, ks, vs, qt, kt, vt,
-    gs, sgt, sg, pt, gt, rt, e01, e20, e21, weave,
-    stage1, recv1, stage2, recv2,
-    in_sem, send1, recv1_sem, send2, recv2_sem,
+    mid, gs, sgt, sg, pt, gt, rt, e01, e20, e21, weave,
+    stage1, recv1, stage2,
+    in_sem, mid_sem, send1, recv1_sem, send2, recv2_sem, line_sem,
 ):
     loads = []
     order = ((cot_h, cot), (wos_h, wos), (qs_h, qs), (ks_h, ks), (vs_h, vs), (w_h, w), (wot_h, wot), (qt_h, qt), (kt_h, kt), (vt_h, vt))
@@ -143,12 +175,7 @@
         loads.append(copy)
     enter()
 
-    row = lax.broadcasted_iota(jnp.int32, (2 * FRAMES, TOKENS), 0)
-    col = lax.broadcasted_iota(jnp.int32, (2 * FRAMES, TOKENS), 1)
-    half, index = row & 1, row >> 1
-    e01[...] = (col == 3 * index + half).astype(F32).astype(BF16)
-    e20[...] = ((col == 3 * index + 2) & (half == 0)).astype(F32).astype(BF16)
-    e21[...] = ((col == 3 * index + 2) & (half == 1)).astype(F32).astype(BF16)
+    picks(e01, e20, e21)
     row = lax.broadcasted_iota(jnp.int32, (2 * FRAMES, 2 * FRAMES), 0)
     col = lax.broadcasted_iota(jnp.int32, (2 * FRAMES, 2 * FRAMES), 1)
     weave[...] = (col == (row & 1) * FRAMES + (row >> 1)).astype(F32).astype(BF16)
@@ -156,6 +183,7 @@
     loads[0].wait()
     loads[1].wait()
     gs[...] = nt(wos[...], cot[...]).astype(BF16)
+    lines_entered(line_sem.at[0])
     for i in (2, 3, 4):
         loads[i].wait()
 
@@ -174,24 +202,27 @@
         return carry
 
     lax.fori_loop(0, PAIRS, spatial, 0)
+    planes_entered(line_sem)
     sg[...] = sgt[...].T
     loads[5].wait()
 
     def project(n, carry):
         cols = pl.ds(pl.multiple_of(n * 384, 128), 384)
-        mid_o[:, cols] = (cot[:, cols].astype(F32) + nn(sg[...], w[:, cols])).astype(BF16)
+        mid[:, cols] = (cot[:, cols].astype(F32) + nn(sg[...], w[:, cols])).astype(BF16)
         return carry
 
     lax.fori_loop(0, FEATURES // 384, project, 0)
+    keep = pltpu.make_async_copy(mid, mid_o, mid_sem)
+    keep.start()
     loads[6].wait()
-    entered()
-
-    low = nt(mid_o[...], wot[0:256]).astype(BF16)
+    entered(line_sem.at[1])
+
+    low = nt(mid[...], wot[0:256]).astype(BF16)
     stage1[0] = nn(e01[...], low[:, 0:128]).astype(BF16)
     stage1[1] = nn(e01[...], low[:, 128:256]).astype(BF16)
     stage1[2] = (nn(e20[...], low[:, 0:128]) + nn(e21[...], low[:, 128:256])).astype(BF16)
     send(stage1, recv1, send1, recv1_sem.at[0], *CHUNKS1[0])
-    high = nt(mid_o[...], wot[256:576]).astype(BF16)
+    high = nt(mid[...], wot[256:576]).astype(BF16)
     stage1[3] = nn(e01[...], high[:, 0:128]).astype(BF16)
     stage1[4] = nn(e01[...], high[:, 128:256]).astype(BF16)
     stage1[5] = (nn(e20[...], high[:, 0:128]) + nn(e21[...], high[:, 128:256])).astype(BF16)
@@ -270,6 +301,25 @@
             pack2(t, t // 3 * 2)
         send(stage2, recv2, send2, recv2_sem.at[p], lo, hi)
 
+    for p in range(PAIRS):
+        arrived(recv2, recv2_sem.at[p], *CHUNKS2[p])
+    keep.wait()
+    sent(stage1, send1)
+    sent(stage2, send2)
+
+
+def finish(mid_h, recv_h, mid_o, out_o, recv, out, mid, e01, e20, e21, in_sem, mid_sem, out_sem):
+    fetch = pltpu.make_async_copy(mid_h, mid, mid_sem.at[0])
+    keep = pltpu.make_async_copy(mid, mid_o, mid_sem.at[1])
+    loads = [
+        pltpu.make_async_copy(recv_h.at[t : t + 3], recv.at[t : t + 3], in_sem.at[t // 3])
+        for t in range(0, SLOTS2, 3)
+    ]
+    for load in loads:
+        load.start()
+    fetch.start()
+    picks(e01, e20, e21)
+
     def put(c, block):
         start, width = c * 128, block.shape[0]
         at = start
@@ -278,23 +328,31 @@
             stop = min((unit + 1) * PAIR, start + width)
             p, kind = unit // 3, unit % 3
             dest = kind * CH + p * PAIR + at - unit * PAIR
-            out_o[dest : dest + stop - at] = block[at - start : stop - start]
+            out[dest : dest + stop - at] = block[at - start : stop - start]
             at = stop
 
-    def unpack2(t, c):
+    stores = []
+    for t in range(0, SLOTS2, 3):
+        loads[t // 3].wait()
+        if t == 6:
+            fetch.wait()
+            keep.start()
+        c = t // 3 * 2
         wide = min(128, 3 * CH - (c + 1) * 128)
-        pair = recv2[t + 2]
-        put(c, (tn(recv2[t], e01[...]) + tn(pair, e20[...])).astype(BF16))
-        last = (tn(recv2[t + 1], e01[...]) + tn(pair, e21[...])).astype(BF16)
+        pair = recv[t + 2]
+        put(c, (tn(recv[t], e01[...]) + tn(pair, e20[...])).astype(BF16))
+        last = (tn(recv[t + 1], e01[...]) + tn(pair, e21[...])).astype(BF16)
         put(c + 1, last[:wide])
-
-    for p in range(PAIRS):
-        lo, hi = CHUNKS2[p]
-        arrived(recv2, recv2_sem.at[p], lo, hi)
-        for t in range(lo, hi, 3):
-            unpack2(t, t // 3 * 2)
-    sent(stage1, send1)
-    sent(stage2, send2)
+        for p in range(PAIRS):
+            if c * 128 < 3 * PAIR * (p + 1) <= (c + 2) * 128:
+                for kind in range(3):
+                    rows = pl.ds(kind * CH + p * PAIR, PAIR)
+                    copy = pltpu.make_async_copy(out.at[rows], out_o.at[rows], out_sem.at[p * 3 + kind])
+                    copy.start()
+                    stores.append(copy)
+    keep.wait()
+    for copy in stores:
+        copy.wait()
 
 
 def local(cot, wos, wqkv, wot, qs, ks, vs, qt, kt, vt):
@@ -304,19 +362,18 @@
     def turn(a):
         return jnp.transpose(a, (1, 2, 0))
 
-    vmem = pl.BlockSpec(memory_space=pltpu.VMEM)
     hbm = pl.BlockSpec(memory_space=pl.ANY)
     spatial = pltpu.VMEM((CH, TOKENS), BF16)
     temporal = pltpu.VMEM((POS, CH, FRAMES), BF16)
     pick = pltpu.VMEM((2 * FRAMES, TOKENS), BF16)
-    middle, grads = pl.pallas_call(
+    middle, blocks = pl.pallas_call(
         kernel,
         out_shape=(
             jax.ShapeDtypeStruct((TOKENS, FEATURES), BF16),
-            jax.ShapeDtypeStruct((3 * CH, TOKENS), BF16),
+            jax.ShapeDtypeStruct((SLOTS2, 2 * FRAMES, 128), BF16),
         ),
         in_specs=[hbm] * 10,
-        out_specs=(vmem, vmem),
+        out_specs=(hbm, hbm),
         scratch_shapes=[
             pltpu.VMEM((TOKENS, FEATURES), BF16),
             pltpu.VMEM((CH, FEATURES), BF16),
@@ -324,6 +381,7 @@
             pltpu.VMEM((CH, FEATURES), BF16),
             spatial, spatial, spatial,
             temporal, temporal, temporal,
+            pltpu.VMEM((TOKENS, FEATURES), BF16),
             spatial,
             pltpu.VMEM((3 * CH, TOKENS), BF16),
             pltpu.VMEM((TOKENS, 3 * CH), BF16),
@@ -335,12 +393,13 @@
             pltpu.VMEM((SLOTS1, 2 * FRAMES, 128), BF16),
             pltpu.VMEM((SLOTS1, 2 * FRAMES, 128), BF16),
             pltpu.VMEM((SLOTS2, 2 * FRAMES, 128), BF16),
-            pltpu.VMEM((SLOTS2, 2 * FRAMES, 128), BF16),
             pltpu.SemaphoreType.DMA((10,)),
+            pltpu.SemaphoreType.DMA,
             pltpu.SemaphoreType.DMA,
             pltpu.SemaphoreType.DMA((len(CHUNKS1),)),
             pltpu.SemaphoreType.DMA,
             pltpu.SemaphoreType.DMA((len(CHUNKS2),)),
+            pltpu.SemaphoreType.REGULAR((2,)),
         ],
         compiler_params=pltpu.CompilerParams(
             collective_id=0, has_side_effects=True, vmem_limit_bytes=56 << 20
@@ -351,6 +410,26 @@
         flip(qs), flip(ks), flip(vs),
         turn(qt), turn(kt), turn(vt),
     )
+    middle, grads = pl.pallas_call(
+        finish,
+        out_shape=(
+            jax.ShapeDtypeStruct((TOKENS, FEATURES), BF16),
+            jax.ShapeDtypeStruct((3 * CH, TOKENS), BF16),
+        ),
+        in_specs=[hbm] * 2,
+        out_specs=(hbm, hbm),
+        scratch_shapes=[
+            pltpu.VMEM((SLOTS2, 2 * FRAMES, 128), BF16),
+            pltpu.VMEM((3 * CH, TOKENS), BF16),
+            pltpu.VMEM((TOKENS, FEATURES), BF16),
+            pick, pick, pick,
+            pltpu.SemaphoreType.DMA((SLOTS2 // 3,)),
+            pltpu.SemaphoreType.DMA((2,)),
+            pltpu.SemaphoreType.DMA((3 * PAIRS,)),
+        ],
+        compiler_params=pltpu.CompilerParams(vmem_limit_bytes=56 << 20),
+        name="unpack",
+    )(middle, blocks)
     return middle[None], grads.T[None]
 
 

time: 82.4 us -> 72.9 us (0.88)
  Pallas kernels: 77.7 us -> 71 us
  local copies, waits for them, and re-layouts: 3.32 us -> 0 us
    pallas_call x1, Pallas kernels: 77.7 us -> 66.8 us  [local(): pl.pallas_call(kernel, out_shape=(jax.ShapeDtypeStruct((TOKENS, FEATURES)...]
    pallas_call x0 -> x1, Pallas kernels: none -> 4.25 us  [local(): pl.pallas_call(finish, out_shape=(jax.ShapeDtypeStruct((TOKENS, FEATURES)...]
    unnamed x4 -> x0, local copies, waits for them, and re-layouts: 3.32 us -> none
where the time goes in v2:
time: 72.9 us; the launch traced here: 71.7 us
  Pallas kernels  71 us (97%)
    pallas_call x1, Pallas kernels, local(): pl.pallas_call(kernel, out_shape=(jax.ShapeDtypeStruct((TOKENS, FEATURES)...  66.8 us
    pallas_call x1, Pallas kernels, local(): pl.pallas_call(finish, out_shape=(jax.ShapeDtypeStruct((TOKENS, FEATURES)...  4.25 us

profile of v2, /device:TPU:32, one launch (start us, length us, event | category | flops | bytes accessed | tf_op | source)
XLA Modules:
  0.0 71.7 jit_solution(12715127967899583531)
XLA Ops:
  0.6 66.8 %reward_backward.1 = (bf16[384,1152]{1,0:T(8,128)(2,1)}, bf16[21,256,128]{2,1,0:T(8,128)(2,1)}) custom-call(bf16[384,1152]{1,0:T(8,128)(2,1)} %bitcast.19, bf16[576,1152]{1,0:T(8,128)(2,1)} %wos_h.1, bf16[1728,1152]{1,0:T(8,128)(2,1)} %bitcast.18, bf16[576,1152]{1,0:T(8,128)(2,1)} %wot_h.1, bf16[576,384]{1,0:T(8,128)(2,1)} %bitcast.20, ...), custom_call_target="tpu_custom_call" | custom-call | tf_op jit(solution)/shard_map/reward_backward/pallas_call | solution.py:369
  67.4 4.2 %unpack.1 = (bf16[384,1152]{1,0:T(8,128)(2,1)}, bf16[1728,384]{1,0:T(8,128)(2,1)}) custom-call(bf16[384,1152]{1,0:T(8,128)(2,1)} %get-tuple-element.6.mid_h, bf16[21,256,128]{2,1,0:T(8,128)(2,1)} %get-tuple-element.7.recv_h), custom_call_target="tpu_custom_call" | custom-call | tf_op jit(solution)/shard_map/unpack/pallas_call | solution.py:413

commit v3 on v2

v3 whole, which is shorter than its diff:
```python
import functools

import jax
import jax.numpy as jnp
from jax import lax
from jax.experimental import pallas as pl
from jax.experimental.pallas import tpu as pltpu
from jax.sharding import PartitionSpec as P

HEADS = 8
HEAD = 72
CH = HEADS * HEAD
GROUPS = ((0, 3), (3, 6), (6, 8))
TOKENS = 384
FRAMES = 128
POS = 3
FEATURES = 1152
SLOTS = 4
AHEAD = 3
SLOTS1 = 7
SLOTS2 = 21
CHUNKS1 = ((0, 3), (3, 7))
CHUNKS2 = ((0, 6), (6, 15), (15, 21))
LAST = CHUNKS2[-1][0]
SPLIT = (432, 432, 416)
SCALE = HEAD ** -0.5
LOG2E = 1.4426950408889634
F32 = jnp.float32
BF16 = jnp.bfloat16


def dot(a, b, ca, cb):
    return lax.dot_general(a, b, (((ca,), (cb,)), ((), ())), preferred_element_type=F32)


def nn(a, b):
    return dot(a, b, 1, 0)


def nt(a, b):
    return dot(a, b, 1, 1)


def tn(a, b):
    return dot(a, b, 0, 0)


def coords():
    outer, inner = lax.axis_index("outer"), lax.axis_index("inner")
    y = outer * 2 + lax.div(inner, 32)
    z = lax.rem(lax.div(inner, 4), 8)
    x = lax.rem(inner, 4)
    return y, z, x


def device(y, z, x):
    return lax.axis_index("sample") * FRAMES + (y * 8 + z) * 4 + x


def my_index():
    return lax.axis_index("outer") * 64 + lax.axis_index("inner")


def greet(sem, line):
    y, z, x = coords()
    if line == "x":
        peers = [(y, z, lax.rem(x + i, 4)) for i in range(1, 4)]
    elif line == "y":
        peers = [(lax.rem(y + i, 4), z, x) for i in range(1, 4)]
    else:
        peers = [(y, lax.rem(z + i, 8), x) for i in range(1, 8)]
    for peer in peers:
        pl.semaphore_signal(
            sem, inc=1, device_id=device(*peer), device_id_type=pl.DeviceIdType.LOGICAL
        )


def enter():
    barrier = pltpu.get_barrier_semaphore()
    for line in "zyx":
        greet(barrier, line)


def lines_entered(sem):
    pl.semaphore_wait(pltpu.get_barrier_semaphore(), 13)
    greet(sem, "x")


def planes_entered(sems):
    pl.semaphore_wait(sems.at[0], 3)
    greet(sems.at[1], "y")


def entered(sem):
    pl.semaphore_wait(sem, 3)


def send(stage, recv, send_sem, recv_sem, lo, hi):
    me = my_index()
    sample = lax.axis_index("sample")
    y, z, x = coords()
    sign = 1 - 2 * sample
    depth = [lax.rem(z + sign * i + 8, 8) * 4 for i in range(8)]
    land = recv.at[lo:hi, pl.ds(pl.multiple_of(me * 2, 2), 2)]
    pltpu.make_async_copy(stage.at[lo:hi, pl.ds(pl.multiple_of(me * 2, 2), 2)], land, recv_sem).start()

    def one(across, away):
        ty = lax.rem(y + sign * lax.div(across, 4) + 4, 4)
        tx = lax.rem(x + sign * lax.rem(across, 4) + 4, 4)
        index = ty * 32 + depth[away] + tx
        pltpu.make_async_remote_copy(
            src_ref=stage.at[lo:hi, pl.ds(pl.multiple_of(index * 2, 2), 2)],
            dst_ref=land,
            send_sem=send_sem,
            recv_sem=recv_sem,
            device_id=sample * FRAMES + index,
            device_id_type=pl.DeviceIdType.LOGICAL,
        ).start()

    def body(turn, carry):
        for i, away in enumerate((4, 1, 7, 2, 6, 3, 5)):
            one(lax.rem(turn + 5 * i + 5, 16), away)
        one(turn + 1, 0)
        return carry

    lax.fori_loop(0, 15, body, 0)
    for i, away in enumerate((4, 1, 7, 2, 6, 3, 5)):
        one((15 + 5 * i + 5) % 16, away)


def arrived(recv, sem, lo, hi):
    pltpu.make_async_copy(recv.at[lo:hi], recv.at[lo:hi], sem).wait()


def sent(stage, sem):
    part = stage.at[:, : 2 * (FRAMES - 1)]
    pltpu.make_async_copy(part, part, sem).wait()


def softmax_t(scores):
    top = jnp.max(scores, axis=0, keepdims=True)
    weights = jnp.exp2((scores - top) * (SCALE * LOG2E))
    return weights * (1.0 / jnp.sum(weights, axis=0, keepdims=True))


def score_grad(weights, grad_weight):
    inner = jnp.sum(weights * grad_weight, axis=0, keepdims=True)
    return (weights * (grad_weight - inner)).astype(BF16)


def unpack2(recv, e01, e20, e21, out, lo, hi):
    def put(c, block):
        at, stop = c * 128, c * 128 + block.shape[0]
        for first, last in GROUPS:
            size = (last - first) * HEAD
            for kind in range(3):
                start = 3 * first * HEAD + kind * size
                a, b = max(at, start), min(stop, start + size)
                if a < b:
                    dest = kind * CH + first * HEAD + a - start
                    out[dest : dest + b - a] = block[a - at : b - at]

    for t in range(lo, hi, 3):
        c = t // 3 * 2
        wide = min(128, 3 * CH - (c + 1) * 128)
        pair = recv[t + 2]
        put(c, (tn(recv[t], e01[...]) + tn(pair, e20[...])).astype(BF16))
        last = (tn(recv[t + 1], e01[...]) + tn(pair, e21[...])).astype(BF16)
        put(c + 1, last[:wide])


def picks(e01, e20, e21):
    row = lax.broadcasted_iota(jnp.int32, (2 * FRAMES, TOKENS), 0)
    col = lax.broadcasted_iota(jnp.int32, (2 * FRAMES, TOKENS), 1)
    half, index = row & 1, row >> 1
    e01[...] = (col == 3 * index + half).astype(F32).astype(BF16)
    e20[...] = ((col == 3 * index + 2) & (half == 0)).astype(F32).astype(BF16)
    e21[...] = ((col == 3 * index + 2) & (half == 1)).astype(F32).astype(BF16)


def kernel(
    cot_h, wos_h, w_h, wot_h, qs_h, ks_h, vs_h, qt_h, kt_h, vt_h,
    mid, recv2, picked, part,
    cot, wos, w, wot, qs, ks, vs, qt, kt, vt,
    gs, sgt, sg, pt, gt, rt, weave,
    score, grad_weight, weight_low, grad_score, stage1, recv1, stage2,
    in_sem, send1, recv1_sem, send2, recv2_sem, line_sem,
):
    loads = []
    order = ((qs_h, qs), (ks_h, ks), (cot_h, cot), (wos_h, wos), (vs_h, vs), (w_h, w), (wot_h, wot), (qt_h, qt), (kt_h, kt), (vt_h, vt))
    for i, (src, dst) in enumerate(order):
        loads.append(pltpu.make_async_copy(src, dst, in_sem.at[i]))
    for copy in loads[:5]:
        copy.start()
    enter()

    e01, e20, e21 = (picked.at[i] for i in range(3))
    picks(e01, e20, e21)
    row = lax.broadcasted_iota(jnp.int32, (2 * FRAMES, 2 * FRAMES), 0)
    col = lax.broadcasted_iota(jnp.int32, (2 * FRAMES, 2 * FRAMES), 1)
    weave[...] = (col == (row & 1) * FRAMES + (row >> 1)).astype(F32).astype(BF16)

    def scores(h):
        rows = slice(h * HEAD, (h + 1) * HEAD)
        score[h % SLOTS] = tn(ks[rows], qs[rows])

    def weight_grads(h):
        rows = slice(h * HEAD, (h + 1) * HEAD)
        grad_weight[h % 2] = tn(vs[rows], gs[rows])

    def soften(h):
        weights = softmax_t(score[h % SLOTS])
        score[h % SLOTS] = weights
        weight_low[h % SLOTS] = weights.astype(BF16)

    def weigh(h):
        grad_score[h % 2] = score_grad(score[h % SLOTS], grad_weight[h % 2])

    def gather(h):
        rows = slice(h * HEAD, (h + 1) * HEAD)
        parts = (
            nn(ks[rows], grad_score[h % 2]) * SCALE,
            nt(qs[rows], grad_score[h % 2]) * SCALE,
            nt(gs[rows], weight_low[h % SLOTS]),
        )
        for kind, part in enumerate(parts):
            sgt[kind * CH + h * HEAD : kind * CH + (h + 1) * HEAD] = part.astype(BF16)

    loads[0].wait()
    loads[1].wait()
    for h in range(AHEAD):
        scores(h)
    loads[2].wait()
    loads[3].wait()
    for copy in loads[5:7]:
        copy.start()
    gs[...] = nt(wos[...], cot[...]).astype(BF16)
    for h in range(AHEAD):
        soften(h)
    lines_entered(line_sem.at[0])
    for copy in loads[7:]:
        copy.start()
    loads[4].wait()
    for step in range(HEADS + 2):
        if AHEAD <= step + 1 < HEADS:
            scores(step + 1)
        if step < HEADS:
            weight_grads(step)
        if AHEAD <= step < HEADS:
            soften(step)
        if 0 <= step - 1 < HEADS:
            weigh(step - 1)
        if 0 <= step - 2 < HEADS:
            gather(step - 2)
            done = (step - 1) * HEAD
            for block in range(0, 3 * CH, 128):
                stop = min(block + 128, 3 * CH)
                need = max(min(stop - kind * CH, CH) for kind in range(3) if block < (kind + 1) * CH and stop > kind * CH)
                if done - HEAD < need <= done:
                    sg[:, block:stop] = sgt[block:stop].T
    planes_entered(line_sem)
    loads[5].wait()

    for n in range(0, FEATURES, 256):
        cols = slice(n, min(n + 256, FEATURES))
        mid[:, cols] = (cot[:, cols].astype(F32) + nn(sg[...], w[:, cols])).astype(BF16)
    loads[6].wait()
    entered(line_sem.at[1])

    low = nt(mid[...], wot[0:256]).astype(BF16)
    stage1[0] = nn(e01[...], low[:, 0:128]).astype(BF16)
    stage1[1] = nn(e01[...], low[:, 128:256]).astype(BF16)
    stage1[2] = (nn(e20[...], low[:, 0:128]) + nn(e21[...], low[:, 128:256])).astype(BF16)
    send(stage1, recv1, send1, recv1_sem.at[0], *CHUNKS1[0])
    high = nt(mid[...], wot[256:576]).astype(BF16)
    stage1[3] = nn(e01[...], high[:, 0:128]).astype(BF16)
    stage1[4] = nn(e01[...], high[:, 128:256]).astype(BF16)
    stage1[5] = (nn(e20[...], high[:, 0:128]) + nn(e21[...], high[:, 128:256])).astype(BF16)
    rest = high[:, 256:320]
    stage1[6] = jnp.concatenate([nn(e01[...], rest), nn(e20[...], rest)], axis=1).astype(BF16)
    send(stage1, recv1, send1, recv1_sem.at[1], *CHUNKS1[1])

    for i in (7, 8, 9):
        loads[i].wait()

    def prepare(j, carry):
        for first in (0, 4):
            cuts = [slice(h * HEAD, (h + 1) * HEAD) for h in range(first, first + 4)]
            parts = [tn(kt[j, cut], qt[j, cut]) for cut in cuts]
            for i, part in enumerate(parts):
                pt[j, first + i] = softmax_t(part)
        return carry

    lax.fori_loop(0, POS, prepare, 0)

    def unpack1(base, c):
        for i in range(2):
            block = tn(recv1[base + i], weave[...]).astype(BF16)
            rows = slice((c + i) * 128, (c + i + 1) * 128)
            gt[0, rows] = block[:, :128]
            gt[1, rows] = block[:, 128:]
        block = tn(recv1[base + 2], weave[...]).astype(BF16)
        gt[2, c * 128 : (c + 1) * 128] = block[:, :128]
        gt[2, (c + 1) * 128 : (c + 2) * 128] = block[:, 128:]

    def temporal(lo, hi):
        def body(j, carry):
            heads = range(lo, hi)
            cuts = [slice(h * HEAD, (h + 1) * HEAD) for h in heads]
            weights = [pt[j, h] for h in heads]
            grads = [tn(vt[j, cut], gt[j, cut]) for cut in cuts]
            values = [nt(gt[j, cut], w.astype(BF16)) for cut, w in zip(cuts, weights)]
            scores = [score_grad(w, g) for w, g in zip(weights, grads)]
            queries = [nn(kt[j, cut], g) * SCALE for cut, g in zip(cuts, scores)]
            keys = [nt(qt[j, cut], g) * SCALE for cut, g in zip(cuts, scores)]
            size = (hi - lo) * HEAD
            for kind, parts in enumerate((queries, keys, values)):
                start = 3 * lo * HEAD + kind * size
                rt[j, start : start + size] = jnp.concatenate(parts, axis=0).astype(BF16)
            return carry

        lax.fori_loop(0, POS, body, 0)

    def pack2(t, c):
        wide = min(128, 3 * CH - (c + 1) * 128)
        for i, width in ((0, 128), (1, wide)):
            rows = slice((c + i) * 128, (c + i) * 128 + width)
            both = jnp.concatenate([rt[0, rows], rt[1, rows]], axis=1)
            stage2[t + i, :, 0:width] = nt(weave[...], both).astype(BF16)
        first = nt(weave[:, :128], rt[2, c * 128 : (c + 1) * 128])
        second = nt(weave[:, 128:], rt[2, (c + 1) * 128 : (c + 1) * 128 + wide])
        if wide < 128:
            second = jnp.concatenate([second, jnp.zeros((2 * FRAMES, 128 - wide), F32)], axis=1)
        stage2[t + 2] = (first + second).astype(BF16)

    def exchange(g):
        temporal(*GROUPS[g])
        lo, hi = CHUNKS2[g]
        for t in range(lo, hi, 3):
            pack2(t, t // 3 * 2)
        send(stage2, recv2, send2, recv2_sem.at[g], lo, hi)

    arrived(recv1, recv1_sem.at[0], *CHUNKS1[0])
    unpack1(0, 0)
    exchange(0)
    arrived(recv1, recv1_sem.at[1], *CHUNKS1[1])
    unpack1(3, 2)
    block = tn(recv1[6], weave[...]).astype(BF16)
    gt[0, 512:576] = block[:64, :128]
    gt[1, 512:576] = block[:64, 128:]
    gt[2, 512:576] = block[64:, :128]
    for g in range(1, len(GROUPS)):
        exchange(g)

    for g, (lo, hi) in enumerate(CHUNKS2):
        arrived(recv2, recv2_sem.at[g], lo, hi)
        if lo < LAST:
            unpack2(recv2, e01, e20, e21, part, lo, hi)
    sent(stage1, send1)
    sent(stage2, send2)


def finish(mid, recv, picked, part, mid_o, out_o, out, mid_sem, out_sem):
    keep = pltpu.make_async_copy(mid, mid_o, mid_sem)
    keep.start()
    stores = []

    def store(src, kind, lo, hi):
        rows = pl.ds(kind * CH + lo, hi - lo)
        copy = pltpu.make_async_copy(src.at[rows], out_o.at[rows], out_sem.at[len(stores)])
        copy.start()
        stores.append(copy)

    for kind in range(3):
        store(part, kind, 0, SPLIT[kind])
    unpack2(recv, *(picked.at[i] for i in range(3)), out, LAST, SLOTS2)
    for kind in range(3):
        store(out, kind, SPLIT[kind], CH)
    keep.wait()
    for copy in stores:
        copy.wait()


def local(cot, wos, wqkv, wot, qs, ks, vs, qt, kt, vt):
    def flip(a):
        return a[0].T

    def turn(a):
        return jnp.transpose(a, (1, 2, 0))

    hbm = pl.BlockSpec(memory_space=pl.ANY)
    vmem = pl.BlockSpec(memory_space=pltpu.VMEM)
    spatial = pltpu.VMEM((CH, TOKENS), BF16)
    temporal = pltpu.VMEM((POS, CH, FRAMES), BF16)
    middle, blocks, picked, part = pl.pallas_call(
        kernel,
        out_shape=(
            pltpu.VMEM((TOKENS, FEATURES), BF16),
            pltpu.VMEM((SLOTS2, 2 * FRAMES, 128), BF16),
            pltpu.VMEM((3, 2 * FRAMES, TOKENS), BF16),
            pltpu.VMEM((3 * CH, TOKENS), BF16),
        ),
        in_specs=[hbm] * 10,
        out_specs=(vmem, vmem, vmem, vmem),
        scratch_shapes=[
            pltpu.VMEM((TOKENS, FEATURES), BF16),
            pltpu.VMEM((CH, FEATURES), BF16),
            pltpu.VMEM((3 * CH, FEATURES), BF16),
            pltpu.VMEM((CH, FEATURES), BF16),
            spatial, spatial, spatial,
            temporal, temporal, temporal,
            spatial,
            pltpu.VMEM((3 * CH, TOKENS), BF16),
            pltpu.VMEM((TOKENS, 3 * CH), BF16),
            pltpu.VMEM((POS, HEADS, FRAMES, FRAMES), F32),
            temporal,
            pltpu.VMEM((POS, 3 * CH, FRAMES), BF16),
            pltpu.VMEM((2 * FRAMES, 2 * FRAMES), BF16),
            pltpu.VMEM((SLOTS, TOKENS, TOKENS), F32),
            pltpu.VMEM((2, TOKENS, TOKENS), F32),
            pltpu.VMEM((SLOTS, TOKENS, TOKENS), BF16),
            pltpu.VMEM((2, TOKENS, TOKENS), BF16),
            pltpu.VMEM((SLOTS1, 2 * FRAMES, 128), BF16),
            pltpu.VMEM((SLOTS1, 2 * FRAMES, 128), BF16),
            pltpu.VMEM((SLOTS2, 2 * FRAMES, 128), BF16),
            pltpu.SemaphoreType.DMA((10,)),
            pltpu.SemaphoreType.DMA,
            pltpu.SemaphoreType.DMA((len(CHUNKS1),)),
            pltpu.SemaphoreType.DMA,
            pltpu.SemaphoreType.DMA((len(CHUNKS2),)),
            pltpu.SemaphoreType.REGULAR((2,)),
        ],
        compiler_params=pltpu.CompilerParams(
            collective_id=0, has_side_effects=True, vmem_limit_bytes=56 << 20
        ),
        name="reward_backward",
    )(
        cot[0], wos, wqkv.T, wot,
        flip(qs), flip(ks), flip(vs),
        turn(qt), turn(kt), turn(vt),
    )
    middle, grads = pl.pallas_call(
        finish,
        out_shape=(
            jax.ShapeDtypeStruct((TOKENS, FEATURES), BF16),
            jax.ShapeDtypeStruct((3 * CH, TOKENS), BF16),
        ),
        in_specs=[vmem] * 4,
        out_specs=(hbm, hbm),
        scratch_shapes=[
            pltpu.VMEM((3 * CH, TOKENS), BF16),
            pltpu.SemaphoreType.DMA,
            pltpu.SemaphoreType.DMA((6,)),
        ],
        compiler_params=pltpu.CompilerParams(vmem_limit_bytes=16 << 20),
        name="unpack",
    )(middle, blocks, picked, part)
    return middle[None], grads.T[None]


def solution(mesh):
    frames = P(("sample", "outer", "inner"), None, None)
    positions = P("sample", ("outer", "inner"), None)
    return jax.shard_map(
        local,
        mesh=mesh,
        in_specs=(frames, P(), P(), P(), frames, frames, frames, positions, positions, positions),
        out_specs=(frames, frames),
        check_vma=False,
    )
```

time: 72.9 us -> 63.4 us (0.87); the launches traced: 71.7 us -> 63.3 us
  Pallas kernels: 71 us -> 62.5 us
    pallas_call x1, Pallas kernels: 66.8 us -> 61.1 us  [local(): pl.pallas_call(kernel, out_shape=(pltpu.VMEM((TOKENS, FEATURES), BF16), p...]
    pallas_call x1, Pallas kernels: 4.25 us -> 1.4 us  [local(): pl.pallas_call(finish, out_shape=(jax.ShapeDtypeStruct((TOKENS, FEATURES)...]
where the time goes in v3:
time: 63.4 us; the launch traced here: 63.3 us
  Pallas kernels  62.5 us (99%)
  between operations  0.8 us (1%)
    pallas_call x1, Pallas kernels, local(): pl.pallas_call(kernel, out_shape=(pltpu.VMEM((TOKENS, FEATURES), BF16), p...  61.1 us
    pallas_call x1, Pallas kernels, local(): pl.pallas_call(finish, out_shape=(jax.ShapeDtypeStruct((TOKENS, FEATURES)...  1.4 us

profile of v3, /device:TPU:32, one launch (start us, length us, event | category | flops | bytes accessed | tf_op | source)
XLA Modules:
  0.0 63.3 jit_solution(6403218187340111315)
XLA Ops:
  0.6 61.1 %reward_backward.1 = (bf16[384,1152]{1,0:T(8,128)(2,1)S(1)}, bf16[21,256,128]{2,1,0:T(8,128)(2,1)S(1)}, bf16[3,256,384]{2,1,0:T(8,128)(2,1)S(1)}, bf16[1728,384]{1,0:T(8,128)(2,1)S(1)}) custom-call(bf16[384,1152]{1,0:T(8,128)(2,1)} %bitcast.19, bf16[576,1152]{1,0:T(8,128)(2,1)} %wos_h.1, bf16[1728,1152]{1,0:T(8,128)(2,1)} %bitcast.18, ...), custom_call_target="tpu_custom_call" | custom-call | tf_op jit(solution)/shard_map/reward_backward/pallas_call | solution.py:395
  61.8 1.4 %unpack.1 = (bf16[384,1152]{1,0:T(8,128)(2,1)}, bf16[1728,384]{1,0:T(8,128)(2,1)}) custom-call(bf16[384,1152]{1,0:T(8,128)(2,1)S(1)} %get-tuple-element.8.mid, bf16[21,256,128]{2,1,0:T(8,128)(2,1)S(1)} %get-tuple-element.9.recv, bf16[3,256,384]{2,1,0:T(8,128)(2,1)S(1)} %get-tuple-element.10.picked, bf16[1728,384]{1,0:T(8,128)(2,1)S(1)} %get-tuple-element.11.part), custom_call_target="tpu_custom_call" | custom-call | tf_op jit(solution)/shard_map/unpack/pallas_call | solution.py:442

commit v4 on v3

--- a/solution.py
+++ b/solution.py
@@ -218,13 +218,9 @@
 
     def gather(h):
         rows = slice(h * HEAD, (h + 1) * HEAD)
-        parts = (
-            nn(ks[rows], grad_score[h % 2]) * SCALE,
-            nt(qs[rows], grad_score[h % 2]) * SCALE,
-            nt(gs[rows], weight_low[h % SLOTS]),
-        )
-        for kind, part in enumerate(parts):
-            sgt[kind * CH + h * HEAD : kind * CH + (h + 1) * HEAD] = part.astype(BF16)
+        sgt[rows] = (nn(ks[rows], grad_score[h % 2]) * SCALE).astype(BF16)
+        sg[:, CH + h * HEAD : CH + (h + 1) * HEAD] = (nt(grad_score[h % 2], qs[rows]) * SCALE).astype(BF16)
+        sg[:, 2 * CH + h * HEAD : 2 * CH + (h + 1) * HEAD] = nt(weight_low[h % SLOTS], gs[rows]).astype(BF16)
 
     loads[0].wait()
     loads[1].wait()
@@ -253,10 +249,9 @@
         if 0 <= step - 2 < HEADS:
             gather(step - 2)
             done = (step - 1) * HEAD
-            for block in range(0, 3 * CH, 128):
-                stop = min(block + 128, 3 * CH)
-                need = max(min(stop - kind * CH, CH) for kind in range(3) if block < (kind + 1) * CH and stop > kind * CH)
-                if done - HEAD < need <= done:
+            for block in range(0, CH, 128):
+                stop = min(block + 128, CH)
+                if done - HEAD < stop <= done:
                     sg[:, block:stop] = sgt[block:stop].T
     planes_entered(line_sem)
     loads[5].wait()
@@ -410,7 +405,7 @@
             spatial, spatial, spatial,
             temporal, temporal, temporal,
             spatial,
-            pltpu.VMEM((3 * CH, TOKENS), BF16),
+            spatial,
             pltpu.VMEM((TOKENS, 3 * CH), BF16),
             pltpu.VMEM((POS, HEADS, FRAMES, FRAMES), F32),
             temporal,

time: 63.4 us -> 63.2 us (level)
  no operation moved by 1% of the time
where the time goes in v4:
time: 63.2 us; the launch traced here: 63.1 us
  Pallas kernels  62.3 us (99%)
  between operations  0.8 us (1%)
    pallas_call x1, Pallas kernels, local(): pl.pallas_call(kernel, out_shape=(pltpu.VMEM((TOKENS, FEATURES), BF16), p...  60.9 us
    pallas_call x1, Pallas kernels, local(): pl.pallas_call(finish, out_shape=(jax.ShapeDtypeStruct((TOKENS, FEATURES)...  1.4 us

profile of v4, /device:TPU:32, one launch (start us, length us, event | category | flops | bytes accessed | tf_op | source)
XLA Modules:
  0.0 63.1 jit_solution(8638376510677607198)
XLA Ops:
  0.6 60.9 %reward_backward.1 = (bf16[384,1152]{1,0:T(8,128)(2,1)S(1)}, bf16[21,256,128]{2,1,0:T(8,128)(2,1)S(1)}, bf16[3,256,384]{2,1,0:T(8,128)(2,1)S(1)}, bf16[1728,384]{1,0:T(8,128)(2,1)S(1)}) custom-call(bf16[384,1152]{1,0:T(8,128)(2,1)} %bitcast.19, bf16[576,1152]{1,0:T(8,128)(2,1)} %wos_h.1, bf16[1728,1152]{1,0:T(8,128)(2,1)} %bitcast.18, ...), custom_call_target="tpu_custom_call" | custom-call | tf_op jit(solution)/shard_map/reward_backward/pallas_call | solution.py:390
  61.5 1.4 %unpack.1 = (bf16[384,1152]{1,0:T(8,128)(2,1)}, bf16[1728,384]{1,0:T(8,128)(2,1)}) custom-call(bf16[384,1152]{1,0:T(8,128)(2,1)S(1)} %get-tuple-element.8.mid, bf16[21,256,128]{2,1,0:T(8,128)(2,1)S(1)} %get-tuple-element.9.recv, bf16[3,256,384]{2,1,0:T(8,128)(2,1)S(1)} %get-tuple-element.10.picked, bf16[1728,384]{1,0:T(8,128)(2,1)S(1)} %get-tuple-element.11.part), custom_call_target="tpu_custom_call" | custom-call | tf_op jit(solution)/shard_map/unpack/pallas_call | solution.py:437

commit v5 on v4

--- a/solution.py
+++ b/solution.py
@@ -263,8 +263,9 @@
     entered(line_sem.at[1])
 
     low = nt(mid[...], wot[0:256]).astype(BF16)
-    stage1[0] = nn(e01[...], low[:, 0:128]).astype(BF16)
-    stage1[1] = nn(e01[...], low[:, 128:256]).astype(BF16)
+    both = nn(e01[...], low).astype(BF16)
+    stage1[0] = both[:, :128]
+    stage1[1] = both[:, 128:]
     stage1[2] = (nn(e20[...], low[:, 0:128]) + nn(e21[...], low[:, 128:256])).astype(BF16)
     send(stage1, recv1, send1, recv1_sem.at[0], *CHUNKS1[0])
     high = nt(mid[...], wot[256:576]).astype(BF16)

time: 63.2 us -> 63.1 us (level)
  no operation moved by 1% of the time
where the time goes in v5:
time: 63.1 us; the launch traced here: 63 us
  Pallas kernels  62.2 us (99%)
  between operations  0.8 us (1%)
    pallas_call x1, Pallas kernels, local(): pl.pallas_call(kernel, out_shape=(pltpu.VMEM((TOKENS, FEATURES), BF16), p...  60.8 us
    pallas_call x1, Pallas kernels, local(): pl.pallas_call(finish, out_shape=(jax.ShapeDtypeStruct((TOKENS, FEATURES)...  1.4 us

profile of v5, /device:TPU:32, one launch (start us, length us, event | category | flops | bytes accessed | tf_op | source)
XLA Modules:
  0.0 63.0 jit_solution(10904651733133676331)
XLA Ops:
  0.6 60.8 %reward_backward.1 = (bf16[384,1152]{1,0:T(8,128)(2,1)S(1)}, bf16[21,256,128]{2,1,0:T(8,128)(2,1)S(1)}, bf16[3,256,384]{2,1,0:T(8,128)(2,1)S(1)}, bf16[1728,384]{1,0:T(8,128)(2,1)S(1)}) custom-call(bf16[384,1152]{1,0:T(8,128)(2,1)} %bitcast.19, bf16[576,1152]{1,0:T(8,128)(2,1)} %wos_h.1, bf16[1728,1152]{1,0:T(8,128)(2,1)} %bitcast.18, ...), custom_call_target="tpu_custom_call" | custom-call | tf_op jit(solution)/shard_map/reward_backward/pallas_call | solution.py:391
  61.4 1.4 %unpack.1 = (bf16[384,1152]{1,0:T(8,128)(2,1)}, bf16[1728,384]{1,0:T(8,128)(2,1)}) custom-call(bf16[384,1152]{1,0:T(8,128)(2,1)S(1)} %get-tuple-element.8.mid, bf16[21,256,128]{2,1,0:T(8,128)(2,1)S(1)} %get-tuple-element.9.recv, bf16[3,256,384]{2,1,0:T(8,128)(2,1)S(1)} %get-tuple-element.10.picked, bf16[1728,384]{1,0:T(8,128)(2,1)S(1)} %get-tuple-element.11.part), custom_call_target="tpu_custom_call" | custom-call | tf_op jit(solution)/shard_map/unpack/pallas_call | solution.py:438
